TPU v7x, 128 devices: a whole 4x4x4 slice. The times are simulated.
128 devices in a mesh: seq: 8 (over x_hi, z), doc: 16 (over x_lo, y, core).
Axes of the slice: x: 4 (x_hi: 2, x_lo: 2; x = x_hi * 2 + x_lo), y: 4, z: 4, core: 2. Of those that a mesh axis runs over, the one named last changes fastest.
Arguments:
- hidden_in: bfloat16 [16, 1024, 2880], P('doc', 'seq'), may hold values from -6 to 6
- queries: bfloat16 [16, 1024, 4096], P('doc', 'seq'), may hold values from -8 to 8
- key_heads: bfloat16 [16, 1024, 512], P('doc', 'seq'), may hold values from -8 to 8
- values: bfloat16 [16, 1024, 512], P('doc', 'seq'), may hold values from -6 to 6
- doc_lengths: int32 [16], P('doc'), may hold values from 1 to 1024, 10240 in all
- out_weight: bfloat16 [4096, 2880], P('seq'), may hold values from -0.75 to 0.75
- norm_gain: bfloat16 [2880], replicated, may hold values from 0.099609375 to 1.8984375
- router_weight: bfloat16 [2880, 64], replicated, may hold values from -0.109375 to 0.109375
- expert_ids: int32 [16, 1024, 4], P('doc', 'seq'), may hold values from 0 to 63, all different within a row; in each aligned block of 128 rows (0 to 127, 128 to 255, ..., all dimensions but the last counted through in order) at most 12 rows name the same one
- gate_weight: bfloat16 [128, 2880, 768], P(('seq', 'doc')), may hold values from -0.109375 to 0.109375
- up_weight: bfloat16 [128, 2880, 768], P(('seq', 'doc')), may hold values from -0.109375 to 0.109375
- down_weight: bfloat16 [128, 768, 2880], P(('seq', 'doc')), may hold values from -0.15625 to 0.15625
Outputs:
- layer_out: bfloat16 [16, 1024, 2880], P('doc', 'seq')
Inputs may be any that keep to these rules, and one draw needn't show every extreme that they name: `doc_lengths`: the lengths sum to 10240, and the longest is 1024. `expert_ids`: each token names 4 different experts. Among the 128 positions that one device holds (aligned blocks of a document), no expert is named more than 12 times, and in some such block an expert is named exactly 12 times.
All inputs are finite; a program needn't handle non-finite values. No bound on the sum of `doc_lengths` on one device may be relied on, other than what follows from the above.
Results may differ from a plain program's by a relative error of at most 0.02.
Values may be sent and summed in bfloat16 or wider, within the bound.
No kernel may reach another device: no remote copies, remote signals or barrier semaphores. Data moves between devices by JAX's collectives and lax.ppermute only.
A program may use at most 128 MiB of HBM per device.

v0:
```python
import jax
import jax.numpy as jnp
from jax import lax
from jax.sharding import PartitionSpec as P

HEADS = 64
KVH = 8
HD = 64
TOP = 4
negative_fill = -1e30
swiglu_alpha = 1.702
norm_eps = 1e-05


def rounded(tensor_in):
    return lax.optimization_barrier(tensor_in.astype(jnp.bfloat16))


def local(
    hidden_in,
    queries,
    key_heads,
    values,
    doc_lengths,
    out_weight,
    norm_gain,
    router_weight,
    expert_ids,
    gate_weight,
    up_weight,
    down_weight,
):
    tokens_dev = hidden_in.shape[1]
    model_width = hidden_in.shape[2]
    doc_length = doc_lengths[0]
    group_size = HEADS // KVH
    score_scale = HD ** (-0.5)
    own_queries = queries[0].reshape(tokens_dev, KVH, group_size, HD)
    query_pos = lax.axis_index("seq") * tokens_dev + jnp.arange(tokens_dev, dtype=jnp.int32)
    run_top = jnp.full((KVH, group_size, tokens_dev), negative_fill, jnp.float32)
    piece_keys = lax.all_gather(key_heads, "seq", axis=1, tiled=True)
    piece_values = lax.all_gather(values, "seq", axis=1, tiled=True)
    piece_rows = piece_keys.shape[1]
    key_block = piece_keys[0].reshape(piece_rows, KVH, HD)
    value_block = piece_values[0].reshape(piece_rows, KVH, HD)
    key_pos = jnp.arange(piece_rows, dtype=jnp.int32)
    allowed = (key_pos[None, :] <= query_pos[:, None]) & (key_pos[None, :] < doc_length)
    scores = (
        jnp.einsum("qkgd,jkd->kgqj", own_queries, key_block, preferred_element_type=jnp.float32)
        * score_scale
    )
    scores = jnp.where(allowed, scores, negative_fill)
    new_top = jnp.maximum(run_top, jnp.max(scores, axis=-1))
    weights = jnp.where(allowed, jnp.exp(scores - new_top[..., None]), 0.0)
    new_total = jnp.sum(weights, axis=-1)
    update = jnp.einsum(
        "kgqj,jkd->kgqd",
        weights.astype(jnp.bfloat16),
        value_block,
        preferred_element_type=jnp.float32,
    )
    own_out = (update / new_total[..., None]).astype(jnp.bfloat16)
    own_out = own_out.transpose(2, 0, 1, 3).reshape(1, tokens_dev, HEADS * HD)
    attended = lax.all_to_all(own_out, "seq", split_axis=2, concat_axis=1, tiled=True)[0]
    attention_sum = lax.psum_scatter(
        jnp.dot(attended, out_weight, preferred_element_type=jnp.float32).astype(jnp.bfloat16),
        "seq",
        scatter_dimension=0,
        tiled=True,
    ).astype(jnp.float32)
    residual = rounded(hidden_in[0].astype(jnp.float32) + attention_sum).astype(jnp.float32)
    mean_square = jnp.mean(residual * residual, axis=-1, keepdims=True)
    normed = (residual * lax.rsqrt(mean_square + norm_eps) * norm_gain.astype(jnp.float32)).astype(
        jnp.bfloat16
    )
    logits = jnp.dot(normed, router_weight, preferred_element_type=jnp.float32)
    expert_count = router_weight.shape[1]
    chosen_ids = expert_ids[0]
    expert_range = jnp.arange(expert_count, dtype=jnp.int32)
    matches = chosen_ids[:, :, None] == expert_range[None, None, :]
    chosen_logits = jnp.sum(jnp.where(matches, logits[:, None, :], 0.0), axis=-1)
    raised = jnp.exp(chosen_logits)
    route_share = raised / jnp.sum(raised, axis=-1, keepdims=True)
    capacity = 2 * (tokens_dev * TOP * 3 // (4 * expert_count))
    flat_ids = chosen_ids.reshape(-1)
    one_hot = (flat_ids[:, None] == expert_range[None, :]).astype(jnp.int32)
    slot_rank = jnp.sum(jnp.cumsum(one_hot, axis=0) * one_hot, axis=1) - 1
    dest_row = flat_ids * capacity + slot_rank
    pair_count = tokens_dev * TOP
    slot_table = (
        jnp.full((expert_count * capacity,), tokens_dev, jnp.int32)
        .at[dest_row]
        .set(jnp.arange(pair_count, dtype=jnp.int32) // TOP)
    )
    padded = jnp.concatenate([normed, jnp.zeros((1, model_width), jnp.bfloat16)], axis=0)
    outgoing = padded[slot_table].reshape(expert_count, capacity, model_width)
    doubled = jnp.broadcast_to(outgoing[:, None], (expert_count, 2, capacity, model_width)).reshape(
        2 * expert_count, capacity, model_width
    )
    arrived = lax.all_to_all(doubled, ("seq", "doc"), split_axis=0, concat_axis=0, tiled=True)
    flat_rows = arrived.reshape(-1, model_width)
    gate_val = jnp.dot(flat_rows, gate_weight[0], preferred_element_type=jnp.float32)
    up_val = jnp.dot(flat_rows, up_weight[0], preferred_element_type=jnp.float32)
    active = (gate_val * jax.nn.sigmoid(swiglu_alpha * gate_val) * (up_val + 1.0)).astype(
        jnp.bfloat16
    )
    arrived_back = lax.all_to_all(
        jnp.dot(active, down_weight[0], preferred_element_type=jnp.float32)
        .astype(jnp.bfloat16)
        .reshape(arrived.shape),
        ("seq", "doc"),
        split_axis=0,
        concat_axis=0,
        tiled=True,
    )
    arrived_back = arrived_back.reshape(expert_count, 2, capacity, model_width)
    expert_out = rounded(
        arrived_back[:, 0].astype(jnp.float32) + arrived_back[:, 1].astype(jnp.float32)
    )
    expert_out = expert_out.reshape(expert_count * capacity, model_width)
    gathered = expert_out[dest_row].reshape(tokens_dev, TOP, model_width)
    mixture_sum = jnp.einsum("tk,tkd->td", route_share, gathered.astype(jnp.float32))
    layer_out = (residual + mixture_sum).astype(jnp.bfloat16)
    return layer_out[None]


def solution(mesh):
    in_specs = (
        P("doc", "seq", None),
        P("doc", "seq", None),
        P("doc", "seq", None),
        P("doc", "seq", None),
        P("doc"),
        P("seq", None),
        P(),
        P(),
        P("doc", "seq", None),
        P(("seq", "doc"), None, None),
        P(("seq", "doc"), None, None),
        P(("seq", "doc"), None, None),
    )
    out_specs = P("doc", "seq", None)
    return jax.shard_map(local, mesh=mesh, in_specs=in_specs, out_specs=out_specs, check_vma=False)
```

profile of v0, /device:TPU:32, one launch (start us, length us, event | category | flops | bytes accessed | tf_op | source)
XLA Modules:
  0.0 778.7 jit_solution(9515316538338982292)
XLA Ops:
  11.2 46.7 %all-gather.3.cloned.1.call-done = bf16[1,1024,512]{2,1,0:T(8,128)(2,1)} async-done(((bf16[1,128,512]{2,1,0:T(8,128)(2,1)}), bf16[1,1024,512]{2,1,0:T(8,128)(2,1)}) %all-gather.3.cloned.1.call-update) | async-done | bytes 1048592 | tf_op jit(solution)/shard_map/all_gather | solution.py:41
  60.1 14.7 %fusion = (f32[8,8,128]{2,1,0:T(8,128)S(1)}, f32[8,1024,128,8]{2,1,3,0:T(8,128)}) fusion(pred[128,1024]{0,1:T(8,128)(4,1)S(1)} %fusion.27, bf16[1024,8,64,1]{0,2,3,1:T(8,128)(2,1)} %bitcast.110, bf16[128,8,8,64]{0,3,2,1:T(8,128)(2,1)} %bitcast.109), kind=kOutput, calls=%fused_computation.5 | convolution fusion | flops 1098899456 | bytes 35815424 | tf_op jit(solution)/shard_map/qkgd,jkd->kgqj/dot_general | solution.py:49
  74.8 14.9 %fusion.1 = f32[8,8,128]{2,1,0:T(8,128)S(1)} fusion(f32[8,1024,128,8]{2,1,3,0:T(8,128)} %get-tuple-element.6, f32[8,8,128]{2,1,0:T(8,128)S(1)} %broadcast_maximum_fusion, pred[128,1024]{0,1:T(8,128)(4,1)S(1)} %fusion.27), kind=kLoop, calls=%fused_computation.6 | loop fusion | flops 41934848 | bytes 33751040 | tf_op jit(solution)/shard_map/reduce_sum | solution.py:55
  89.7 15.7 %all-gather.5.cloned.1.call-done = bf16[1,1024,512]{2,1,0:T(8,128)(2,1)} async-done(((bf16[1,128,512]{2,1,0:T(8,128)(2,1)}), bf16[1,1024,512]{2,1,0:T(8,128)(2,1)}) %all-gather.5.cloned.1.call-update) | async-done | bytes 1048592 | tf_op jit(solution)/shard_map/all_gather | solution.py:42
  107.7 14.5 %fusion.18 = bf16[128,8,8,64]{0,3,2,1:T(8,128)(2,1)S(1)} fusion(bf16[1024,8,64,1]{0,2,3,1:T(8,128)(2,1)} %bitcast.113, f32[8,1024,128,8]{2,1,3,0:T(8,128)} %get-tuple-element.6, f32[8,8,128]{2,1,0:T(8,128)S(1)} %broadcast_maximum_fusion, pred[128,1024]{0,1:T(8,128)(4,1)S(1)} %fusion.27, f32[128,8,8]{0,2,1:T(8,128)S(1)} %bitcast.115), kind=kOutput, calls=%fused_computation.28 | convolution fusion | flops 1116733440 | bytes 35848192 | tf_op jit(solution)/shard_map/kgqj,jkd->kgqd/dot_general | solution.py:56
  122.2 17.3 %copy.101 = bf16[1,128,4096]{1,0,2:T(2,128)(2,1)} copy(bf16[1,128,4096]{1,2,0:T(8,128)(2,1)S(1)} %bitcast.112) | data formatting | bytes 2097152 | tf_op jit(solution)/shard_map/reshape | solution.py:63
  140.1 24.4 %reduce.2 = bf16[4096,128]{1,0:T(8,128)(2,1)} reduce(bf16[4096,1,128]{2,1,0:T(2,128)(2,1)} %bitcast.108, bf16[]{:T(256)} %broadcast.127), dimensions={1}, to_apply=%bitcast.104.reduce_sub_computation | reduce | bytes 2097154
  166.7 19.9 %all_to_all.25 = bf16[8,2,32768]{2,1,0:T(2,128)(2,1)} all-to-all(bf16[8,2,32768]{2,1,0:T(2,128)(2,1)} %reshape.147), channel_id=1, replica_groups=mesh['seq'=8,'doc'=16] {'seq'}, dimensions={0} | all-to-all | bytes 2097152 | tf_op jit(solution)/shard_map/all_to_all | solution.py:64
  197.4 6.3 convolution_convert_fusion.1
  203.7 8.5 %copy.90 = bf16[1024,2880]{1,0:T(8,128)(2,1)} copy(bf16[1024,2880]{0,1:T(8,128)(2,1)} %convolution_convert_fusion.1) | data formatting | bytes 11796480
  218.0 88.8 %reduce-scatter.4.cloned.1.call-done = bf16[128,2880]{1,0:T(8,128)(2,1)} async-done(((bf16[1024,2880]{1,0:T(8,128)(2,1)}), bf16[128,2880]{1,0:T(8,128)(2,1)}) %reduce-scatter.4.cloned.1.call-update) | async-done | bytes 737296 | tf_op jit(solution)/shard_map/reduce_scatter | solution.py:65
  314.2 7.3 broadcast_in_dim.65
  326.0 143.3 %all_to_all.26 = bf16[128,12,2880]{2,1,0:T(8,128)(2,1)} all-to-all(bf16[128,12,2880]{2,1,0:T(8,128)(2,1)S(1)} %bitcast.106), channel_id=1, replica_groups=mesh['seq'=8,'doc'=16] {'seq','doc'}, dimensions={0} | all-to-all | bytes 17694720 | tf_op jit(solution)/shard_map/all_to_all | solution.py:100
  469.3 14.6 %reshape.107 = bf16[1536,2880]{1,0:T(8,128)(2,1)} reshape(bf16[128,12,2880]{2,1,0:T(8,128)(2,1)} %all_to_all.26) | data formatting | bytes 17694720 | tf_op jit(solution)/shard_map/reshape | solution.py:101
  483.9 12.7 %fusion.8 = f32[1536,768]{1,0:T(8,128)} fusion(bf16[1536,2880]{1,0:T(8,128)(2,1)} %reshape.107, bf16[1,2880,768]{2,1,0:T(8,128)(2,1)} %param.22), kind=kOutput, calls=%fused_computation.18 | convolution fusion | flops 6794772480 | bytes 17989632 | tf_op jit(solution)/shard_map/dot_general | solution.py:103
  496.6 23.8 %convolution_convert_fusion = bf16[1536,2880]{0,1:T(8,128)(2,1)} fusion(bf16[1,768,2880]{1,2,0:T(8,128)(2,1)} %param.23, f32[1536,768]{1,0:T(8,128)} %fusion.8, bf16[1536,2880]{1,0:T(8,128)(2,1)} %reshape.107, bf16[1,2880,768]{2,1,0:T(8,128)(2,1)} %param.21), kind=kOutput, calls=%fused_computation.11 | convolution fusion | flops 13603405824 | bytes 31260672 | tf_op jit(solution)/shard_map/dot_general | solution.py:108
  520.4 12.5 %copy.81 = bf16[1536,2880]{1,0:T(8,128)(2,1)} copy(bf16[1536,2880]{0,1:T(8,128)(2,1)} %convolution_convert_fusion) | data formatting | bytes 17694720 | tf_op jit(solution)/shard_map/convert_element_type | solution.py:109
  532.8 13.5 %reshape.108 = bf16[128,12,2880]{2,1,0:T(8,128)(2,1)} reshape(bf16[1536,2880]{1,0:T(8,128)(2,1)} %copy.81) | data formatting | bytes 17694720 | tf_op jit(solution)/shard_map/reshape | solution.py:110
  546.3 14.6 %all-to-all-start.2 = ((bf16[128,12,2880]{2,1,0:T(8,128)(2,1)}), bf16[128,12,2880]{2,1,0:T(8,128)(2,1)}, u32[]{:S(2)}, u32[]{:S(2)}) async-start(bf16[128,12,2880]{2,1,0:T(8,128)(2,1)} %reshape.108), calls=%async_computation.2 | async-start | bytes 24117248 | tf_op jit(solution)/shard_map/all_to_all | solution.py:107
  561.6 171.4 %all-to-all-done.2 = bf16[128,12,2880]{2,1,0:T(8,128)(2,1)} async-done(((bf16[128,12,2880]{2,1,0:T(8,128)(2,1)}), bf16[128,12,2880]{2,1,0:T(8,128)(2,1)}, u32[]{:S(2)}, u32[]{:S(2)}) %all-to-all-start.2) | async-done | bytes 8847392 | tf_op jit(solution)/shard_map/all_to_all | solution.py:107
  733.0 8.5 %fusion.6 = bf16[64,12,2880]{2,1,0:T(8,128)(2,1)} fusion(bf16[64,2,12,2880]{3,2,1,0:T(8,128)(2,1)} %bitcast.24), kind=kLoop, calls=%fused_computation.12 | loop fusion | flops 8847360 | bytes 13271040 | tf_op jit(solution)/shard_map/convert_element_type | solution.py:16
  741.5 7.9 %reshape.110 = bf16[768,2880]{1,0:T(8,128)(2,1)} reshape(bf16[64,12,2880]{2,1,0:T(8,128)(2,1)} %fusion.6) | data formatting | bytes 8847360 | tf_op jit(solution)/shard_map/reshape | solution.py:120
  749.4 9.6 %gather_fusion.1 = bf16[512,2880]{1,0:T(8,128)(2,1)} fusion(bf16[768,2880]{1,0:T(8,128)(2,1)} %reshape.110, s32[1024]{0:T(1024)S(1)} %pad_clamp_fusion), kind=kCustom, calls=%fused_computation.1 | custom fusion | bytes 5900288 | tf_op jit(solution)/shard_map/gather | solution.py:121
  759.0 5.9 reshape.111
  (70 shorter events, 47.1 us)
Async XLA Ops:
  6.5 190.8 %copy-start = (bf16[512,2880]{0,1:T(8,128)(2,1)S(1)}, bf16[512,2880]{0,1:T(8,128)(2,1)}, u32[]{:S(2)}) copy-start(bf16[512,2880]{0,1:T(8,128)(2,1)} %param.17) | copy-start | bytes 8847364
  6.5 51.3 %all-gather.3.cloned.1.call-start = ((), (), s32[]{:S(2)}) async-start(), calls=%async_computation.4 | async-start | bytes 1179648 | tf_op jit(solution)/shard_map/all_gather | solution.py:41
  7.3 98.2 %all-gather.5.cloned.1.call-start = ((), (), s32[]{:S(2)}) async-start(), calls=%async_computation.5 | async-start | bytes 1179648 | tf_op jit(solution)/shard_map/all_gather | solution.py:42
  8.0 298.8 %reduce-scatter.4.cloned.1.call-start = ((), (), s32[]{:S(2)}) async-start(), calls=%async_computation.6 | async-start | bytes 6782976 | tf_op jit(solution)/shard_map/reduce_scatter | solution.py:65
  212.2 0.7 copy-start.6
  212.2 1.1 copy-start.4
  212.2 1.5 copy-start.7
  308.1 0.9 copy-start.2
  546.3 14.7 %copy-start.5 = (bf16[2880,64]{0,1:T(8,128)(2,1)S(1)}, bf16[2880,64]{0,1:T(8,128)(2,1)}, u32[]{:S(2)}) copy-start(bf16[2880,64]{0,1:T(8,128)(2,1)} %param.19) | copy-start | bytes 1105924
  546.3 186.7 %all-to-all-start.2 = ((bf16[128,12,2880]{2,1,0:T(8,128)(2,1)}), bf16[128,12,2880]{2,1,0:T(8,128)(2,1)}, u32[]{:S(2)}, u32[]{:S(2)}) async-start(bf16[128,12,2880]{2,1,0:T(8,128)(2,1)} %reshape.108), calls=%async_computation.2 | async-start | bytes 24117248 | tf_op jit(solution)/shard_map/all_to_all | solution.py:107
  759.0 12.9 %copy-start.1 = (bf16[512,2880]{0,1:T(8,128)(2,1)S(1)}, bf16[512,2880]{0,1:T(8,128)(2,1)}, u32[]{:S(2)}) copy-start(bf16[512,2880]{0,1:T(8,128)(2,1)} %param.17) | copy-start | bytes 8847364
  764.9 3.7 copy-start.3
Sparse Core Ops, SparseCore 0:
  9.7 48.1 all-gather.2
  60.2 45.1 all-gather.4
  212.3 94.4 reduce-scatter.3
where the time goes:
time: 787 us; the launch traced here: 779 us
  waiting for transfers between devices  324 us (41%)
  blocking collectives  163 us (21%)
  local copies, waits for them, and re-layouts  134 us (17%)
  matrix products  76 us (10%)
  other arithmetic  52.3 us (7%)
  starting transfers between devices  14.7 us (2%)
  between operations  14.2 us (2%)
    all_to_all x1, waiting for transfers between devices, local(): lax.all_to_all(jnp.dot(active, down_weight[0], preferred_element_type=jnp...  171 us
    all_to_all x1, blocking collectives, local(): lax.all_to_all(doubled, ('seq', 'doc'), split_axis=0, concat_axis=0, tile...  143 us
    reduce_scatter x1, waiting for transfers between devices, local(): lax.psum_scatter(jnp.dot(attended, out_weight, preferred_element_type=jnp...  88.8 us
    all_gather x1, waiting for transfers between devices, local(): piece_keys = lax.all_gather(key_heads, 'seq', axis=1, tiled=True)  46.7 us
    unnamed x1, other arithmetic  24.4 us
    unnamed x24, local copies, waits for them, and re-layouts  23.8 us
    dot_general x1, matrix products, local(): jnp.dot(active, down_weight[0], preferred_element_type=jnp.float32)  23.8 us
    all_to_all x1, blocking collectives, local(): lax.all_to_all(own_out, 'seq', split_axis=2, concat_axis=1, tiled=True)[0]  19.9 us
  transfers between devices with their start and end apart: 4, of which 4 were waited for; matrix products, arithmetic and copies ran while one was open for 5% of the time, Pallas kernels for 0%

commit v1 on v0

--- a/solution.py
+++ b/solution.py
@@ -10,6 +10,13 @@
 negative_fill = -1e30
 swiglu_alpha = 1.702
 norm_eps = 1e-05
+
+
+def _order_quarters(array_here):
+    return jnp.concatenate(
+        lax.all_to_all(jnp.stack(jnp.split(array_here, lax.axis_size("seq"), axis=2)), "seq", 0, 0),
+        axis=1,
+    )
 
 
 def rounded(tensor_in):
@@ -61,7 +68,7 @@
     )
     own_out = (update / new_total[..., None]).astype(jnp.bfloat16)
     own_out = own_out.transpose(2, 0, 1, 3).reshape(1, tokens_dev, HEADS * HD)
-    attended = lax.all_to_all(own_out, "seq", split_axis=2, concat_axis=1, tiled=True)[0]
+    attended = _order_quarters(own_out)[0]
     attention_sum = lax.psum_scatter(
         jnp.dot(attended, out_weight, preferred_element_type=jnp.float32).astype(jnp.bfloat16),
         "seq",

time: 787 us -> 738 us (0.938)
  other arithmetic: 52.3 us -> 27.8 us
  local copies, waits for them, and re-layouts: 134 us -> 122 us
  waiting for transfers between devices: 324 us -> 314 us
    unnamed x1 -> x0, other arithmetic: 24.4 us -> none
    reshape x1 -> x0, local copies, waits for them, and re-layouts: 17.3 us -> none  [local(): own_out = own_out.transpose(2, 0, 1, 3).reshape(1, tokens_dev, HEADS * HD)]
    all_to_all x1, waiting for transfers between devices: 171 us -> 161 us  [local(): lax.all_to_all(jnp.dot(active, down_weight[0], preferred_element_type=jnp...]
    unnamed x24 -> x35, local copies, waits for them, and re-layouts: 23.8 us -> 29.5 us
where the time goes in v1:
time: 738 us; the launch traced here: 728 us
  waiting for transfers between devices  314 us (43%)
  blocking collectives  162 us (22%)
  local copies, waits for them, and re-layouts  122 us (17%)
  matrix products  74.8 us (10%)
  other arithmetic  27.8 us (4%)
  starting transfers between devices  14 us (2%)
  between operations  14 us (2%)
    all_to_all x1, waiting for transfers between devices, local(): lax.all_to_all(jnp.dot(active, down_weight[0], preferred_element_type=jnp...  161 us
    all_to_all x1, blocking collectives, local(): lax.all_to_all(doubled, ('seq', 'doc'), split_axis=0, concat_axis=0, tile...  143 us
    reduce_scatter x1, waiting for transfers between devices, local(): lax.psum_scatter(jnp.dot(attended, out_weight, preferred_element_type=jnp...  88.8 us
    all_gather x1, waiting for transfers between devices, local(): piece_keys = lax.all_gather(key_heads, 'seq', axis=1, tiled=True)  46.7 us
    unnamed x35, local copies, waits for them, and re-layouts  29.5 us
    dot_general x1, matrix products, local(): jnp.dot(active, down_weight[0], preferred_element_type=jnp.float32)  23.8 us
    all_to_all x1, blocking collectives, _order_quarters(): lax.all_to_all(jnp.stack(jnp.split(array_here, lax.axis_size('seq'), axis...  18.6 us
    all_gather x1, waiting for transfers between devices, local(): piece_values = lax.all_gather(values, 'seq', axis=1, tiled=True)  15.7 us
  transfers between devices with their start and end apart: 4, of which 4 were waited for; matrix products, arithmetic and copies ran while one was open for 5% of the time, Pallas kernels for 0%

profile of v1, /device:TPU:32, one launch (start us, length us, event | category | flops | bytes accessed | tf_op | source)
XLA Modules:
  0.0 728.0 jit_solution(9340210528176750145)
XLA Ops:
  11.2 46.7 %all-gather.3.cloned.1.call-done = bf16[1,1024,512]{2,1,0:T(8,128)(2,1)} async-done(((bf16[1,128,512]{2,1,0:T(8,128)(2,1)}), bf16[1,1024,512]{2,1,0:T(8,128)(2,1)}) %all-gather.3.cloned.1.call-update) | async-done | bytes 1048592 | tf_op jit(solution)/shard_map/all_gather | solution.py:48
  60.1 14.7 %fusion = (f32[8,8,128]{2,1,0:T(8,128)S(1)}, f32[8,1024,128,8]{2,1,3,0:T(8,128)}) fusion(pred[128,1024]{0,1:T(8,128)(4,1)S(1)} %fusion.27, bf16[1024,8,64,1]{0,2,3,1:T(8,128)(2,1)} %bitcast.117, bf16[128,8,8,64]{0,3,2,1:T(8,128)(2,1)} %bitcast.116), kind=kOutput, calls=%fused_computation.5 | convolution fusion | flops 1098899456 | bytes 35815424 | tf_op jit(solution)/shard_map/qkgd,jkd->kgqj/dot_general | solution.py:56
  74.8 14.9 %fusion.1 = f32[8,8,128]{2,1,0:T(8,128)S(1)} fusion(f32[8,1024,128,8]{2,1,3,0:T(8,128)} %get-tuple-element.14, f32[8,8,128]{2,1,0:T(8,128)S(1)} %broadcast_maximum_fusion, pred[128,1024]{0,1:T(8,128)(4,1)S(1)} %fusion.27), kind=kLoop, calls=%fused_computation.6 | loop fusion | flops 41934848 | bytes 33751040 | tf_op jit(solution)/shard_map/reduce_sum | solution.py:62
  89.7 15.7 %all-gather.5.cloned.1.call-done = bf16[1,1024,512]{2,1,0:T(8,128)(2,1)} async-done(((bf16[1,128,512]{2,1,0:T(8,128)(2,1)}), bf16[1,1024,512]{2,1,0:T(8,128)(2,1)}) %all-gather.5.cloned.1.call-update) | async-done | bytes 1048592 | tf_op jit(solution)/shard_map/all_gather | solution.py:49
  107.7 14.5 %fusion.18 = bf16[128,8,8,64]{0,3,2,1:T(8,128)(2,1)S(1)} fusion(bf16[1024,8,64,1]{0,2,3,1:T(8,128)(2,1)} %bitcast.119, f32[8,1024,128,8]{2,1,3,0:T(8,128)} %get-tuple-element.14, f32[8,8,128]{2,1,0:T(8,128)S(1)} %broadcast_maximum_fusion, pred[128,1024]{0,1:T(8,128)(4,1)S(1)} %fusion.27, f32[128,8,8]{0,2,1:T(8,128)S(1)} %bitcast.121), kind=kOutput, calls=%fused_computation.28 | convolution fusion | flops 1116733440 | bytes 35848192 | tf_op jit(solution)/shard_map/kgqj,jkd->kgqd/dot_general | solution.py:63
  140.6 18.6 %all_to_all.15 = bf16[8,1,128,512]{3,2,1,0:T(8,128)(2,1)S(1)} all-to-all(bf16[8,1,128,512]{3,2,1,0:T(8,128)(2,1)} %bitcast_dynamic-update-slice_fusion), channel_id=1, replica_groups=mesh['seq'=8,'doc'=16] {'seq'}, dimensions={0} | all-to-all | bytes 2097152 | tf_op jit(solution)/shard_map/all_to_all | solution.py:17
  159.2 5.1 convolution_convert_fusion.1
  164.3 8.5 %copy.95 = bf16[1024,2880]{1,0:T(8,128)(2,1)} copy(bf16[1024,2880]{0,1:T(8,128)(2,1)} %convolution_convert_fusion.1) | data formatting | bytes 11796480
  178.7 88.8 %reduce-scatter.4.cloned.1.call-done = bf16[128,2880]{1,0:T(8,128)(2,1)} async-done(((bf16[1024,2880]{1,0:T(8,128)(2,1)}), bf16[128,2880]{1,0:T(8,128)(2,1)}) %reduce-scatter.4.cloned.1.call-update) | async-done | bytes 737296 | tf_op jit(solution)/shard_map/reduce_scatter | solution.py:72
  269.9 4.8 gather_fusion
  274.8 7.3 %broadcast_in_dim.65 = bf16[64,12,2880]{2,1,0:T(8,128)(2,1)} reshape(bf16[768,2880]{1,0:T(8,128)(2,1)} %gather_fusion) | data formatting | bytes 8847360 | tf_op jit(solution)/shard_map/broadcast_in_dim | solution.py:104
  282.1 4.5 broadcast_in_dim.66
  286.7 143.4 %all_to_all.16 = bf16[128,12,2880]{2,1,0:T(8,128)(2,1)} all-to-all(bf16[128,12,2880]{2,1,0:T(8,128)(2,1)S(1)} %bitcast.115), channel_id=1, replica_groups=mesh['seq'=8,'doc'=16] {'seq','doc'}, dimensions={0} | all-to-all | bytes 17694720 | tf_op jit(solution)/shard_map/all_to_all | solution.py:107
  430.1 14.6 %reshape.106 = bf16[1536,2880]{1,0:T(8,128)(2,1)} reshape(bf16[128,12,2880]{2,1,0:T(8,128)(2,1)} %all_to_all.16) | data formatting | bytes 17694720 | tf_op jit(solution)/shard_map/reshape | solution.py:108
  444.6 12.7 %fusion.8 = f32[1536,768]{1,0:T(8,128)} fusion(bf16[1536,2880]{1,0:T(8,128)(2,1)} %reshape.106, bf16[1,2880,768]{2,1,0:T(8,128)(2,1)} %param.22), kind=kOutput, calls=%fused_computation.18 | convolution fusion | flops 6794772480 | bytes 17989632 | tf_op jit(solution)/shard_map/dot_general | solution.py:110
  457.3 23.8 %convolution_convert_fusion = bf16[1536,2880]{0,1:T(8,128)(2,1)} fusion(bf16[1,768,2880]{1,2,0:T(8,128)(2,1)} %param.23, f32[1536,768]{1,0:T(8,128)} %fusion.8, bf16[1536,2880]{1,0:T(8,128)(2,1)} %reshape.106, bf16[1,2880,768]{2,1,0:T(8,128)(2,1)} %param.21), kind=kOutput, calls=%fused_computation.11 | convolution fusion | flops 13603405824 | bytes 31260672 | tf_op jit(solution)/shard_map/dot_general | solution.py:115
  481.1 12.5 %copy.86 = bf16[1536,2880]{1,0:T(8,128)(2,1)} copy(bf16[1536,2880]{0,1:T(8,128)(2,1)} %convolution_convert_fusion) | data formatting | bytes 17694720 | tf_op jit(solution)/shard_map/convert_element_type | solution.py:116
  493.6 13.5 %reshape.107 = bf16[128,12,2880]{2,1,0:T(8,128)(2,1)} reshape(bf16[1536,2880]{1,0:T(8,128)(2,1)} %copy.86) | data formatting | bytes 17694720 | tf_op jit(solution)/shard_map/reshape | solution.py:117
  507.0 13.9 %all-to-all-start.2 = ((bf16[128,12,2880]{2,1,0:T(8,128)(2,1)}), bf16[128,12,2880]{2,1,0:T(8,128)(2,1)}, u32[]{:S(2)}, u32[]{:S(2)}) async-start(bf16[128,12,2880]{2,1,0:T(8,128)(2,1)} %reshape.107), calls=%async_computation.2 | async-start | bytes 24117248 | tf_op jit(solution)/shard_map/all_to_all | solution.py:114
  521.6 161.0 %all-to-all-done.2 = bf16[128,12,2880]{2,1,0:T(8,128)(2,1)} async-done(((bf16[128,12,2880]{2,1,0:T(8,128)(2,1)}), bf16[128,12,2880]{2,1,0:T(8,128)(2,1)}, u32[]{:S(2)}, u32[]{:S(2)}) %all-to-all-start.2) | async-done | bytes 8847392 | tf_op jit(solution)/shard_map/all_to_all | solution.py:114
  682.5 8.5 %fusion.6 = bf16[64,12,2880]{2,1,0:T(8,128)(2,1)} fusion(bf16[64,2,12,2880]{3,2,1,0:T(8,128)(2,1)} %bitcast.31), kind=kLoop, calls=%fused_computation.12 | loop fusion | flops 8847360 | bytes 13271040 | tf_op jit(solution)/shard_map/convert_element_type | solution.py:23
  691.0 7.9 %reshape.109 = bf16[768,2880]{1,0:T(8,128)(2,1)} reshape(bf16[64,12,2880]{2,1,0:T(8,128)(2,1)} %fusion.6) | data formatting | bytes 8847360 | tf_op jit(solution)/shard_map/reshape | solution.py:127
  698.9 9.6 %gather_fusion.1 = bf16[512,2880]{1,0:T(8,128)(2,1)} fusion(bf16[768,2880]{1,0:T(8,128)(2,1)} %reshape.109, s32[1024]{0:T(1024)S(1)} %get-tuple-element.15), kind=kCustom, calls=%fused_computation.1 | custom fusion | bytes 5900288 | tf_op jit(solution)/shard_map/gather | solution.py:128
  708.6 5.9 reshape.110
  (79 shorter events, 42.6 us)
Async XLA Ops:
  6.5 152.7 %copy-start = (bf16[512,2880]{0,1:T(8,128)(2,1)S(1)}, bf16[512,2880]{0,1:T(8,128)(2,1)}, u32[]{:S(2)}) copy-start(bf16[512,2880]{0,1:T(8,128)(2,1)} %param.17) | copy-start | bytes 8847364
  6.5 51.3 %all-gather.3.cloned.1.call-start = ((), (), s32[]{:S(2)}) async-start(), calls=%async_computation.4 | async-start | bytes 1179648 | tf_op jit(solution)/shard_map/all_gather | solution.py:48
  7.3 98.2 %all-gather.5.cloned.1.call-start = ((), (), s32[]{:S(2)}) async-start(), calls=%async_computation.5 | async-start | bytes 1179648 | tf_op jit(solution)/shard_map/all_gather | solution.py:49
  8.0 259.4 %reduce-scatter.4.cloned.1.call-start = ((), (), s32[]{:S(2)}) async-start(), calls=%async_computation.6 | async-start | bytes 6782976 | tf_op jit(solution)/shard_map/reduce_scatter | solution.py:72
  172.8 0.7 copy-start.6
  172.8 1.1 copy-start.4
  172.8 1.5 copy-start.7
  268.7 0.9 copy-start.2
  507.0 13.9 %copy-start.5 = (bf16[2880,64]{0,1:T(8,128)(2,1)S(1)}, bf16[2880,64]{0,1:T(8,128)(2,1)}, u32[]{:S(2)}) copy-start(bf16[2880,64]{0,1:T(8,128)(2,1)} %param.19) | copy-start | bytes 1105924
  507.0 175.5 %all-to-all-start.2 = ((bf16[128,12,2880]{2,1,0:T(8,128)(2,1)}), bf16[128,12,2880]{2,1,0:T(8,128)(2,1)}, u32[]{:S(2)}, u32[]{:S(2)}) async-start(bf16[128,12,2880]{2,1,0:T(8,128)(2,1)} %reshape.107), calls=%async_computation.2 | async-start | bytes 24117248 | tf_op jit(solution)/shard_map/all_to_all | solution.py:114
  708.6 12.9 %copy-start.1 = (bf16[512,2880]{0,1:T(8,128)(2,1)S(1)}, bf16[512,2880]{0,1:T(8,128)(2,1)}, u32[]{:S(2)}) copy-start(bf16[512,2880]{0,1:T(8,128)(2,1)} %param.17) | copy-start | bytes 8847364
  714.5 3.7 copy-start.3
Sparse Core Ops, SparseCore 0:
  9.7 48.1 all-gather.2
  60.2 45.1 all-gather.4
  173.0 94.4 reduce-scatter.3
